TPU v7x, 32 devices: a whole 2x2x4 slice. The times are simulated.
32 devices in a mesh: groups: 2 (over x), context: 16 (over z, y, core).
Axes of the slice: x: 2, y: 2, z: 4, core: 2. Of those that a mesh axis runs over, the one named last changes fastest.
Arguments:
- xbc_raw: bfloat16 [4096, 3712], P(('groups', 'context')), parts along dimension 0, may hold values from -6 to 6
- gate_z: bfloat16 [4096, 3584], P(('groups', 'context')), parts along dimension 0, may hold values from -6 to 6
- dt_raw: float32 [4096, 56], P(('groups', 'context')), parts along dimension 0, may hold values from -5 to 5
- a_log: float32 [56], replicated, may hold values from -16 to -2
- conv_weight: float32 [4, 3712], replicated, may hold values from -3 to 3
- norm_gain: float32 [3584], replicated, may hold values from 0.1 to 1.9
- grad_out: bfloat16 [4096, 3584], P(('groups', 'context')), parts along dimension 0, may hold values from -6 to 6
Outputs:
- normed: bfloat16 [4096, 3584], P(('groups', 'context')), parts along dimension 0
- grad_xbc: bfloat16 [4096, 3712], P(('groups', 'context')), parts along dimension 0
- grad_z: bfloat16 [4096, 3584], P(('groups', 'context')), parts along dimension 0
- grad_dt: float32 [4096, 56], P(('groups', 'context')), parts along dimension 0
- grad_conv: float32 [8, 3712], P('groups'), parts along dimension 0
- grad_alog: float32 [112], P('groups'), parts along dimension 0
- grad_gain: float32 [7168], P('groups'), parts along dimension 0
There are 2 independent parts, one for each index of `groups`. A program takes and returns all parts, laid end to end along the dimension named above; an argument that names none is the same for every part. Nothing has to cross between parts.
All inputs are finite; a program needn't handle non-finite values.
Results may differ from a plain program's by a relative error of at most 0.0085.
The roundings to bfloat16 on the way count: a program that leaves them out, or rounds other values in their place, can miss the bound.
Values may be sent and summed in bfloat16 or wider, within the bound.
A program may use at most 128 MiB of HBM per device.

v0:
```python
import functools
import math

import jax
import jax.numpy as jnp
from jax import lax
from jax.experimental import pallas as pl
from jax.experimental.pallas import tpu as pltpu
from jax.sharding import PartitionSpec as P

HEADDIM = 64
DSTATE = 64
LANES = 128
MESH = pl.DeviceIdType.MESH
F32 = jnp.float32
BF16 = jnp.bfloat16
VMEM_LIMIT = 48 * 1024 * 1024


def dot(a, b, ca=1, cb=0):
    return lax.dot_general(a, b, (((ca,), (cb,)), ((), ())), preferred_element_type=F32)


def dot_exact(a, b):
    return jnp.dot(a, b, precision=lax.Precision.HIGHEST, preferred_element_type=F32)


def iota(shape, axis):
    return lax.broadcasted_iota(jnp.int32, shape, axis)


def tile_at(k):
    return pl.ds(pl.multiple_of(k * LANES, LANES), LANES)


def conv_pre(x, halo, taps):
    ext = jnp.concatenate([halo, x], axis=0)
    rows = x.shape[0]
    return ext, sum(taps[o : o + 1] * ext[5 + o : 5 + o + rows] for o in range(4))


def sigmoid(v):
    return 1.0 / (1.0 + jnp.exp(-v))


def steps_of(dt_ref, alog_ref, run_t, step_t):
    raw = dt_ref[...]
    step = jnp.maximum(raw, 0.0) + jnp.log1p(jnp.exp(-jnp.abs(raw)))
    log_decay = -jnp.exp(alog_ref[0:1]) * step
    rows = raw.shape[0]
    tri = (iota((rows, rows), 0) >= iota((rows, rows), 1)).astype(F32)
    running = dot_exact(tri, log_decay)
    run_t[...] = running.T
    step_t[...] = step.T
    return step, log_decay, running


def columns_of(row_ref, k):
    low = jnp.broadcast_to(row_ref[pl.ds(2 * k, 1), :], (LANES, LANES))
    high = jnp.broadcast_to(row_ref[pl.ds(2 * k + 1, 1), :], (LANES, LANES))
    low_t, high_t = low.T, high.T
    return low, high, low_t, high_t, jnp.where(iota((LANES, LANES), 1) < HEADDIM, low_t, high_t)


def pair_weights(run_t, step_t, k):
    low, high, low_t, high_t, spread = columns_of(run_t, k)
    causal = iota((LANES, LANES), 0) >= iota((LANES, LANES), 1)
    gaps = [jnp.where(causal, a - b, -1e30) for a, b in ((low_t, low), (high_t, high))]
    scaled = [jnp.exp(gap) * step_t[pl.ds(2 * k + i, 1), :] for i, gap in enumerate(gaps)]
    return jnp.concatenate(scaled, axis=0), spread


def projections(bc):
    lane = iota(bc.shape, 1)
    turned = pltpu.roll(bc.astype(F32), HEADDIM, 1)
    b_low = jnp.where(lane < DSTATE, bc.astype(F32), 0.0).astype(BF16)
    c_low = jnp.where(lane < DSTATE, turned, 0.0).astype(BF16)
    b_high = jnp.where(lane >= DSTATE, turned, 0.0).astype(BF16)
    return b_low, c_low, b_high


def head_sum(value, k):
    pick = (iota((LANES, LANES), 1) == 2 * k + iota((LANES, LANES), 0) // HEADDIM).astype(BF16)
    high = value.astype(BF16)
    return dot(high, pick) + dot((value - high.astype(F32)).astype(BF16), pick)


def state_tile(ref, k):
    return ref[pl.ds(4 * k, 4)].reshape(DSTATE, LANES)


def forward_kernel(x_ref, halo_ref, dt_ref, alog_ref, w_ref, mix_ref, end_ref, total_ref, lanes_ref, run_t, step_t):
    tiles = x_ref.shape[1] // LANES - 1
    _, _, running = steps_of(dt_ref, alog_ref, run_t, step_t)
    total_ref[...] = jnp.broadcast_to(running[-1:], total_ref.shape)
    lanes_ref[...] = jnp.zeros_like(lanes_ref)

    def mixin(k):
        at = tile_at(k)
        _, pre = conv_pre(x_ref[:, at].astype(F32), halo_ref[:, at], w_ref[:, at])
        mixed = (pre * sigmoid(pre)).astype(BF16)
        mix_ref[:, at] = mixed
        return mixed

    bc = mixin(tiles)

    def body(k, carry):
        mixed = mixin(k)
        spread = columns_of(run_t, k)[-1]
        to_end = jnp.exp(spread[-1:] - spread) * columns_of(step_t, k)[-1]
        lanes_ref[pl.ds(k, 1), :] = spread[-1:]
        ended = dot(bc, (mixed.astype(F32) * to_end).astype(BF16), 0, 0)
        end_ref[pl.ds(4 * k, 4)] = ended[:DSTATE].reshape(4, 16, LANES).astype(BF16)
        return carry

    lax.fori_loop(0, tiles, body, 0)
    spare = end_ref.shape[0] - 4 * tiles
    if spare:
        end_ref[4 * tiles :] = jnp.zeros((spare, 16, LANES), BF16)


def middle_kernel(
    mix_ref, z_ref, dt_ref, alog_ref, gain_ref, out_ref, start_ref,
    normed_ref, gz_ref, gmix_ref, gstart_ref, gain_part_ref, along_ref, gc_ref,
    run_t, step_t, mixer, sums,
):
    inner = z_ref.shape[1]
    tiles = inner // LANES
    steps_of(dt_ref, alog_ref, run_t, step_t)
    bc = mix_ref[:, inner : inner + LANES]
    b_low, c_low, _ = projections(bc)
    scores = dot(c_low, b_low, 1, 1)
    scores2 = jnp.concatenate([scores, scores], axis=0)
    lane = iota((LANES, LANES), 1)
    c_both = jnp.where(lane < DSTATE, c_low.astype(F32), bc.astype(F32)).astype(BF16)

    def parts_of(k):
        start = state_tile(start_ref, k)
        high = start.astype(BF16)
        return jnp.concatenate([(start - high.astype(F32)).astype(BF16), high], axis=0)

    sums[...] = jnp.zeros_like(sums)

    def first(k, carry):
        at = tile_at(k)
        scaled, spread = pair_weights(run_t, step_t, k)
        both = dot((scores2 * scaled).astype(BF16), mix_ref[:, at])
        within = jnp.where(lane < HEADDIM, both[:LANES], both[LANES:])
        carried = dot(c_both, parts_of(k))
        mixed = within + carried * jnp.exp(spread)
        mixer[:, at] = mixed
        z = z_ref[:, at].astype(F32)
        gated = mixed * z * sigmoid(z)
        sums[0] += gated * gated
        sums[1] += gated * out_ref[:, at].astype(F32) * gain_ref[0:1, at]
        return carry

    lax.fori_loop(0, tiles, first, 0)
    scale = lax.rsqrt(jnp.sum(sums[0], axis=1, keepdims=True) / inner + 1e-05)
    back = scale * scale * scale * (jnp.sum(sums[1], axis=1, keepdims=True) / inner)
    along_ref[...] = jnp.zeros_like(along_ref)
    gc_ref[...] = jnp.zeros_like(gc_ref)

    def second(k, carry):
        at = tile_at(k)
        spread = columns_of(run_t, k)[-1]
        mixed = mixer[:, at]
        z = z_ref[:, at].astype(F32)
        gate = sigmoid(z)
        gated = mixed * z * gate
        gain = gain_ref[0:1, at]
        out = out_ref[:, at].astype(F32)
        plain = gated * scale
        normed_ref[:, at] = (plain * gain).astype(BF16)
        gain_row = jnp.sum(out * plain, axis=0, keepdims=True)
        gain_part_ref[k] = jnp.broadcast_to(gain_row, (8, LANES))
        ggated = out * gain * scale - gated * back
        gz_ref[:, at] = (ggated * mixed * gate * (1.0 + z * (1.0 - gate))).astype(BF16)
        exact = ggated * z * gate
        gmixer = exact.astype(BF16)
        gmix_ref[:, at] = exact
        wide = gmixer.astype(F32)
        along_ref[...] += head_sum(wide * mixed, k)
        decayed = exact * jnp.exp(spread)
        high = decayed.astype(BF16)
        low = (decayed - high.astype(F32)).astype(BF16)
        placed = parts_of(k)
        gc_ref[...] += dot(high, placed, 1, 1) + dot(low, placed, 1, 1)
        started = dot(bc, high, 0, 0)
        gstart_ref[pl.ds(4 * k, 4)] = started[DSTATE:].reshape(4, 16, LANES).astype(BF16)
        return carry

    lax.fori_loop(0, tiles, second, 0)
    halves = gc_ref[...]
    gc_ref[...] = jnp.where(lane < DSTATE, 0.0, halves + pltpu.roll(halves, DSTATE, 1))
    spare = gstart_ref.shape[0] - 4 * tiles
    if spare:
        gstart_ref[4 * tiles :] = jnp.zeros((spare, 16, LANES), BF16)


def backward_kernel(
    x_ref, halo_ref, mix_ref, dt_ref, alog_ref, w_ref, gmix_ref, start_ref, gend_ref, gain_part_ref, along_ref, gc_ref,
    gx_ref, head_ref, tail_ref, gdt_ref, part_ref,
    run_t, step_t, gscores, gbc, into, after, carry_rows,
):
    inner = gmix_ref.shape[1]
    tiles = inner // LANES
    step, log_decay, _ = steps_of(dt_ref, alog_ref, run_t, step_t)
    bc = mix_ref[:, inner : inner + LANES]
    b_low, c_low, b_high = projections(bc)
    scores = dot(c_low, b_low, 1, 1)
    scores2 = jnp.concatenate([scores, scores], axis=0)
    lane = iota((LANES, LANES), 1)
    blank = jnp.zeros((DSTATE, LANES), BF16)
    for ref in (gscores, into, after, carry_rows):
        ref[...] = jnp.zeros_like(ref)
    gbc[...] = gc_ref[...]

    def conv_back(k, gmixin):
        at = tile_at(k)
        taps = w_ref[:, at]
        ext, pre = conv_pre(x_ref[:, at].astype(F32), halo_ref[:, at], taps)
        gate = sigmoid(pre)
        gpre = gmixin.astype(BF16).astype(F32) * gate * (1.0 + pre * (1.0 - gate))
        rows = gpre.shape[0]
        none = jnp.zeros((8, LANES), F32)
        padded = jnp.concatenate([none, gpre, none], axis=0)
        gext = sum(taps[o : o + 1] * padded[8 - o : 8 - o + rows + 8] for o in range(4))
        own = gext[3 : 3 + rows]
        gx_ref[:, at] = own.astype(BF16)
        tail_ref[:, at] = own[rows - 16 :]
        head_ref[:, at] = gext[:8]
        return [jnp.sum(gpre * ext[5 + o : 5 + o + rows], axis=0, keepdims=True) for o in range(4)]

    def body(k, carry):
        at = tile_at(k)
        values = mix_ref[:, at]
        gmixer = gmix_ref[:, at]
        scaled, spread = pair_weights(run_t, step_t, k)
        weights = (scores2 * scaled).astype(BF16)
        wide = jnp.concatenate([jnp.where(lane < HEADDIM, gmixer, 0.0), jnp.where(lane < HEADDIM, 0.0, gmixer)], axis=0)
        split = wide.astype(BF16)
        rest = (wide - split.astype(F32)).astype(BF16)
        gweights = (dot(split, values, 1, 1) + dot(rest, values, 1, 1)) * scaled
        gscores[...] += gweights[:LANES] + gweights[LANES:]
        gvalues = dot(weights, split, 0, 0)
        to_end = jnp.exp(spread[-1:] - spread) * columns_of(step_t, k)[-1]
        start, gend = state_tile(start_ref, k), state_tile(gend_ref, k)
        gend_low = jnp.concatenate([gend, blank], axis=0)
        gended = to_end * dot(bc, gend_low)
        values32 = values.astype(F32)
        into[...] += head_sum(values32 * gvalues, k)
        after[...] += head_sum(values32 * gended, k)
        moved = jnp.sum(start * gend.astype(F32), axis=0, keepdims=True) * jnp.exp(spread[-1:])
        carry_rows[...] += head_sum(jnp.broadcast_to(moved, (16, LANES)), k)
        gbc[...] += dot((values32 * to_end).astype(BF16), gend_low, 1, 1)
        taps = conv_back(k, gvalues + gended)
        part_ref[k] = jnp.concatenate(taps + [gain_part_ref[k][:1], jnp.zeros((3, LANES), F32)], axis=0)
        return carry

    lax.fori_loop(0, tiles, body, 0)
    gscore = gscores[...].astype(BF16)
    rest = (gscores[...] - gscore.astype(F32)).astype(BF16)
    from_scores = dot(gscore, c_low, 0, 0) + dot(gscore, b_high) + dot(rest, c_low, 0, 0) + dot(rest, b_high)
    taps = conv_back(tiles, gbc[...] + from_scores)
    rows = step.shape[0]
    later = (iota((rows, rows), 0) <= iota((rows, rows), 1)).astype(F32)
    earlier = (iota((rows, rows), 0) > iota((rows, rows), 1)).astype(F32)
    glog = dot_exact(later, along_ref[...] - into[...]) + dot_exact(earlier, after[...]) + carry_rows[0:1]
    gstep = (into[...] + after[...]) / step - jnp.exp(alog_ref[0:1]) * glog
    gdt_ref[...] = gstep * sigmoid(dt_ref[...])
    galog = jnp.sum(glog * log_decay, axis=0, keepdims=True)
    part_ref[tiles] = jnp.concatenate(taps + [galog, jnp.zeros((3, LANES), F32)], axis=0)
    spare = part_ref.shape[0] - tiles - 1
    if spare:
        part_ref[tiles + 1 :] = jnp.zeros((spare, 8, LANES), F32)


def greet_all(axis, n):
    me = lax.axis_index(axis)
    barrier = pltpu.get_barrier_semaphore()

    def greet(d, carry):
        pl.semaphore_signal(barrier, inc=1, device_id={axis: lax.rem(me + d, n)}, device_id_type=MESH)
        return carry

    lax.fori_loop(1, n, greet, 0)
    pl.semaphore_wait(barrier, n - 1)
    return me


def to_peer(src, dst, send_sem, recv_sem, axis, peer):
    return pltpu.make_async_remote_copy(
        src_ref=src, dst_ref=dst, send_sem=send_sem, recv_sem=recv_sem,
        device_id={axis: peer}, device_id_type=MESH,
    )


def over_peers(n, action):
    def one(d, carry):
        action(d)
        return carry

    lax.fori_loop(1, n, one, 0)


def exchange_kernel(
    n, axis, reverse, in_ref, lanes_ref, total_ref, out_ref, totals_ref, lanes_near,
    near, joined, held, decays, back, ret, passed, sems,
):
    chips = n // 2
    me = lax.axis_index(axis)
    chip, core = lax.div(me, 2), lax.rem(me, 2)
    sibling = me + 1 - 2 * core
    half = in_ref.shape[0] // 2
    per = half // chips

    def peer(d):
        return 2 * lax.rem(chip + d + chips, chips) + core

    barrier = pltpu.get_barrier_semaphore()
    pl.semaphore_signal(barrier, inc=1, device_id={axis: sibling}, device_id_type=MESH)
    over_peers(chips, lambda d: pl.semaphore_signal(barrier, inc=1, device_id={axis: peer(d)}, device_id_type=MESH))
    pl.semaphore_wait(barrier, chips)

    def block(j):
        return pl.ds(j * per, per)

    mine = core * half
    first = core == (1 if reverse else 0)
    swaps = [to_peer(in_ref.at[pl.ds((1 - core) * half, half)], near, sems.at[0, 0], sems.at[1, 0], axis, sibling)]
    if not reverse:
        swaps.append(to_peer(lanes_ref, lanes_near, sems.at[2, 0], sems.at[3, 0], axis, sibling))
        swaps.append(to_peer(total_ref, totals_ref.at[chips], sems.at[4, 0], sems.at[5, 0], axis, sibling))
    for swap in swaps:
        swap.start()
    for swap in swaps:
        swap.wait()

    def lane_decays(r):
        row = pl.ds(lax.div(mine, 4) + r, 1)
        return jnp.exp(lanes_ref[row, :]), jnp.exp(lanes_near[row, :])

    def join(r, carry):
        own, other = lane_decays(r)
        at = pl.ds(4 * r, 4)
        own_state = in_ref[pl.ds(mine + 4 * r, 4)].astype(F32)
        other_state = near[at].astype(F32)
        summed = own_state * jnp.where(first, other, 1.0) + other_state * jnp.where(first, 1.0, own)
        joined[at] = summed.astype(BF16)
        return carry

    lax.fori_loop(0, half // 4, join, 0)

    def outgoing(d):
        there = lax.rem(chip + d, chips)
        return to_peer(joined.at[block(there)], held.at[d], sems.at[0, d], sems.at[1, d], axis, peer(d))

    def totals_out(d):
        return to_peer(totals_ref.at[0], totals_ref.at[d], sems.at[2, d], sems.at[3, d], axis, peer(d))

    if not reverse:
        totals_ref[0] = total_ref[...] + totals_ref[chips]
        over_peers(chips, lambda d: totals_out(d).start())
    over_peers(chips, lambda d: outgoing(d).start())
    held[0] = joined[block(chip)]
    if not reverse:
        over_peers(chips, lambda d: totals_out(d).wait())
    logs = totals_ref[:chips].reshape(chips * 8, LANES)
    for i in range(per):
        pair = lax.div(mine + chip * per + i, 4)
        pick = iota((LANES, LANES), 0) == 2 * pair + iota((LANES, LANES), 1) // HEADDIM
        decays[:, i] = jnp.exp(dot_exact(logs, pick.astype(F32))).reshape(chips, 8, LANES)
    over_peers(chips, lambda d: outgoing(d).wait())

    def advance(step, state):
        j = chips - 1 - step if reverse else step
        d = lax.rem(chip - j + chips, chips)
        back[lax.rem(j - chip + chips, chips)] = state.astype(back.dtype)
        return decays[d][:, :1] * state + held[d].astype(F32)

    lax.fori_loop(0, chips, advance, jnp.zeros((per, 16, LANES), F32))

    def returning(d):
        return to_peer(back.at[d], ret.at[block(chip)], sems.at[4, d], sems.at[5, d], axis, peer(d))

    def arriving(d):
        there = lax.rem(chip - d + chips, chips)
        return to_peer(back.at[d], ret.at[block(there)], sems.at[4, d], sems.at[5, d], axis, peer(-d))

    over_peers(chips, lambda d: returning(d).start())
    ret[block(chip)] = back[0]
    over_peers(chips, lambda d: returning(d).wait_send())
    over_peers(chips, lambda d: arriving(d).wait_recv())

    def hand(r, carry):
        own, other = lane_decays(r)
        at = pl.ds(4 * r, 4)
        own_state = in_ref[pl.ds(mine + 4 * r, 4)].astype(F32)
        other_state = near[at].astype(F32)
        begun = ret[at].astype(F32)
        moved = jnp.where(first, own, other) * begun + jnp.where(first, own_state, other_state)
        out_ref[pl.ds(mine + 4 * r, 4)] = jnp.where(first, begun, moved).astype(out_ref.dtype)
        passed[at] = jnp.where(first, moved, begun).astype(passed.dtype)
        return carry

    lax.fori_loop(0, half // 4, hand, 0)
    final = to_peer(passed, out_ref.at[pl.ds(mine, half)], sems.at[6, 0], sems.at[7, 0], axis, sibling)
    final.start()
    final.wait_send()
    to_peer(passed, out_ref.at[pl.ds((1 - core) * half, half)], sems.at[6, 0], sems.at[7, 0], axis, sibling).wait_recv()


def total_kernel(n, axis, part_ref, head_ref, out_ref, rows_ref, held, sems):
    me = greet_all(axis, n)
    per = part_ref.shape[0] // n

    def block(j):
        return pl.ds(j * per, per)

    def outgoing(d):
        return to_peer(part_ref.at[block(lax.rem(me + d, n))], held.at[d], sems.at[0, d], sems.at[1, d], axis, lax.rem(me + d, n))

    over_peers(n, lambda d: outgoing(d).start())
    rim = to_peer(head_ref, rows_ref, sems.at[2, 0], sems.at[3, 0], axis, lax.rem(me + n - 1, n))
    rim.start()
    held[0] = part_ref[block(me)]
    over_peers(n, lambda d: outgoing(d).wait())

    def add(d, total):
        return total + held[d]

    held[0] = lax.fori_loop(1, n, add, held[0])
    out_ref[block(me)] = held[0]

    def returning(d):
        return to_peer(held.at[0], out_ref.at[block(me)], sems.at[2, d], sems.at[3, d], axis, lax.rem(me + d, n))

    def arriving(d):
        source = lax.rem(me - d + n, n)
        return to_peer(held.at[0], out_ref.at[block(source)], sems.at[2, d], sems.at[3, d], axis, source)

    over_peers(n, lambda d: returning(d).start())
    over_peers(n, lambda d: returning(d).wait_send())
    over_peers(n, lambda d: arriving(d).wait_recv())
    rim.wait()


def call(kernel, operands, outs, scratch, **params):
    whole = pl.BlockSpec(memory_space=pltpu.VMEM)
    return pl.pallas_call(
        kernel,
        out_shape=[jax.ShapeDtypeStruct(shape, dtype) for shape, dtype in outs],
        in_specs=[whole] * len(operands),
        out_specs=[whole] * len(outs),
        scratch_shapes=scratch,
        compiler_params=pltpu.CompilerParams(vmem_limit_bytes=VMEM_LIMIT, **params),
    )(*operands)


def exchange(axis, n, reverse, tiles, lanes, totals, lanes_near=None):
    chips, half = n // 2, tiles.shape[0] // 2
    per = half // chips
    kept = BF16 if reverse else F32
    near, joined, ret, passed = [pltpu.VMEM((half, 16, LANES), held_as) for held_as in (BF16, BF16, kept, kept)]
    slots, back = [pltpu.VMEM((chips, per, 16, LANES), held_as) for held_as in (BF16, kept)]
    scratch = [
        near, joined, slots, pltpu.VMEM((chips, per, 8, LANES), F32), back, ret, passed,
        pltpu.SemaphoreType.DMA((8, chips)),
    ]
    outs = [(tiles.shape, kept)]
    operands = [tiles, lanes, totals]
    if reverse:
        operands.append(lanes_near)

        def kernel(in_ref, lanes_ref, totals_ref, near_ref, out_ref, *rest):
            exchange_kernel(n, axis, True, in_ref, lanes_ref, None, out_ref, totals_ref, near_ref, *rest)
    else:
        kernel = functools.partial(exchange_kernel, n, axis, False)
        outs += [((chips + 1, 8, LANES), F32), (lanes.shape, F32)]
    return call(kernel, operands, outs, scratch, collective_id=1 + reverse, has_side_effects=True)


def on_device(xbc_raw, gate_z, dt_raw, a_log, conv_weight, norm_gain, grad_out):
    axis = "context"
    n = lax.axis_size(axis)
    rows, inner = gate_z.shape
    channels = xbc_raw.shape[1]
    heads = a_log.shape[0]
    tiles = inner // LANES
    unit = n * 8 // math.gcd(n, 8)
    state_tiles = -(-4 * tiles // unit) * unit
    lane_rows = -(-state_tiles // 32) * 8
    part_tiles = -(-(tiles + 1) // n) * n
    rim = lax.ppermute(xbc_raw[rows - 3 :], axis, [(i, i + 1) for i in range(n - 1)])
    halo = jnp.pad(rim.astype(F32), ((5, 0), (0, 0)))
    dt = jnp.pad(dt_raw, ((0, 0), (0, LANES - heads)))
    alog = jnp.pad(a_log, (0, LANES - heads))[None]
    per_head = [pltpu.VMEM((LANES, rows), F32)] * 2
    square = pltpu.VMEM((rows, LANES), F32)

    mixin, ended, total, lanes = call(
        forward_kernel, (xbc_raw, halo, dt, alog, conv_weight),
        [((rows, channels), BF16), ((state_tiles, 16, LANES), BF16), ((8, LANES), F32), ((lane_rows, LANES), F32)], per_head,
    )
    start, totals, lanes_near = exchange(axis, n, False, ended, lanes, total)
    normed, grad_z, gmixer, gstart, gain_part, along, gc = call(
        middle_kernel, (mixin, gate_z, dt, alog, norm_gain[None], grad_out, start),
        [
            ((rows, inner), BF16), ((rows, inner), BF16), ((rows, inner), F32),
            ((state_tiles, 16, LANES), BF16), ((tiles, 8, LANES), F32), ((rows, LANES), F32),
            ((rows, LANES), F32),
        ],
        per_head + [pltpu.VMEM((rows, inner), F32), pltpu.VMEM((2, rows, LANES), F32)],
    )
    (gend,) = exchange(axis, n, True, gstart, lanes, totals, lanes_near)
    gx, head, tail, gdt, part = call(
        backward_kernel,
        (xbc_raw, halo, mixin, dt, alog, conv_weight, gmixer, start, gend, gain_part, along, gc),
        [
            ((rows, channels), BF16), ((8, channels), F32), ((16, channels), F32),
            ((rows, LANES), F32), ((part_tiles, 8, LANES), F32),
        ],
        per_head + [square] * 4 + [pltpu.VMEM((16, LANES), F32)],
    )
    sums, back_rows = call(
        functools.partial(total_kernel, n, axis), (part, head),
        [((part_tiles, 8, LANES), F32), ((8, channels), F32)],
        [pltpu.VMEM((n, part_tiles // n, 8, LANES), F32), pltpu.SemaphoreType.DMA((4, n))],
        collective_id=3, has_side_effects=True,
    )
    borrowed = jnp.where(lax.axis_index(axis) < n - 1, back_rows[:3], 0.0)
    fixed = (tail + jnp.pad(borrowed, ((13, 0), (0, 0)))).astype(BF16)
    grad_xbc = lax.dynamic_update_slice(gx, fixed, (rows - 16, 0))
    conv_total = sums[: tiles + 1, :4].transpose(1, 0, 2).reshape(4, channels)
    return (
        normed, grad_xbc, grad_z, gdt[:, :heads], conv_total,
        sums[tiles, 4, :heads], sums[:tiles, 4].reshape(inner),
    )


def solution(mesh):
    split = P(("groups", "context"), None)
    return jax.shard_map(
        on_device,
        mesh=mesh,
        in_specs=(split, split, split, P(), P(), P(), split),
        out_specs=(split, split, split, split, P("groups", None), P("groups"), P("groups")),
        check_vma=False,
    )
```

profile of v0, /device:TPU:0, one launch (start us, length us, event | category | flops | bytes accessed | tf_op | source)
XLA Modules:
  0.0 119.1 jit_solution(8802825968652271711)
XLA Ops:
  0.6 0.8 slice.18
  1.5 2.4 %collective-permute-start = (bf16[3,3712]{1,0:T(4,128)(2,1)S(1)}, bf16[3,3712]{1,0:T(4,128)(2,1)S(1)}, u32[]{:S(2)}, u32[]{:S(2)}) collective-permute-start(bf16[3,3712]{1,0:T(4,128)(2,1)S(1)} %slice.18), channel_id=1, source_target_pairs={{0,1},{1,2},{2,3},{3,4},{4,5},{5,6},{6,7},{7,8},{8,9},{9,10},{10,1... | collective-permute-start | bytes 66824 | tf_op jit(solution)/shard_map/ppermute | solution.py:495
  3.8 0.7 pad_bitcast_fusion.alog_ref
  4.5 0.8 copy.14
  5.3 0.7 broadcast_in_dim.11.gain_ref
  6.1 0.0 collective-permute-done
  6.1 0.0 copy-start
  6.2 1.2 copy-done
  7.3 0.8 copy-done.5
  8.2 7.9 %shard_map.126 = (bf16[128,3712]{1,0:T(8,128)(2,1)S(1)}, bf16[112,16,128]{2,1,0:T(8,128)(2,1)S(1)}, f32[8,128]{1,0:T(8,128)S(1)}, f32[32,128]{1,0:T(8,128)S(1)}) custom-call(bf16[128,3712]{1,0:T(8,128)(2,1)S(1)} %copy-done, f32[8,3712]{1,0:T(8,128)S(1)} %pad_convert_fusion.halo_ref, f32[128,128]{1,0:T(8,128)S(1)} %pad.20.dt_ref, ...), custom_call_target="tpu_custom_call" | custom-call | tf_op jit(solution)/shard_map/pallas_call | solution.py:451
  16.1 24.8 %shard_map.127 = (f32[112,16,128]{2,1,0:T(8,128)S(1)}, f32[9,8,128]{2,1,0:T(8,128)S(1)}, f32[32,128]{1,0:T(8,128)S(1)}) custom-call(bf16[112,16,128]{2,1,0:T(8,128)(2,1)S(1)} %get-tuple-element.29.in_ref, f32[32,128]{1,0:T(8,128)S(1)} %get-tuple-element.30.lanes_ref, f32[8,128]{1,0:T(8,128)S(1)} %get-tuple-element.31.total_ref), custom_call_target="tpu_custom_call" | custom-call | tf_op jit(solution)/shard_map/pallas_call | solution.py:451
  40.9 0.0 copy-done.3
  40.9 0.0 copy-start.4
  40.9 1.2 copy-done.4
  42.1 16.9 %shard_map.128 = (bf16[128,3584]{1,0:T(8,128)(2,1)}, bf16[128,3584]{1,0:T(8,128)(2,1)}, f32[128,3584]{1,0:T(8,128)}, bf16[112,16,128]{2,1,0:T(8,128)(2,1)S(1)}, ...) custom-call(bf16[128,3712]{1,0:T(8,128)(2,1)S(1)} %get-tuple-element.28.mix_ref, ...), custom_call_target="tpu_custom_call" | custom-call | tf_op jit(solution)/shard_map/pallas_call | solution.py:451
  59.0 23.3 %shard_map.129.gend_ref = bf16[112,16,128]{2,1,0:T(8,128)(2,1)S(1)} custom-call(bf16[112,16,128]{2,1,0:T(8,128)(2,1)S(1)} %get-tuple-element.35.in_ref, f32[32,128]{1,0:T(8,128)S(1)} %get-tuple-element.30.lanes_ref, f32[9,8,128]{2,1,0:T(8,128)S(1)} %get-tuple-element.36.totals_ref, f32[32,128]{1,0:T(8,128)S(1)} %get-tuple-element.37.near_ref), custom_call_target="tpu_custom_call" | custom-call | tf_op jit(solution)/shard_map/pallas_call | solution.py:451
  82.3 1.5 %copy-done.2 = f32[128,3584]{1,0:T(8,128)S(1)} copy-done((f32[128,3584]{1,0:T(8,128)S(1)}, f32[128,3584]{1,0:T(8,128)}, u32[]{:S(2)}) %copy-start.2) | copy-done | bytes 1835032
  83.8 17.7 %shard_map.130 = (bf16[128,3712]{1,0:T(8,128)(2,1)}, f32[8,3712]{1,0:T(8,128)S(1)}, f32[16,3712]{1,0:T(8,128)S(1)}, f32[128,128]{1,0:T(8,128)S(1)}, f32[32,8,128]{2,1,0:T(8,128)S(1)}) custom-call(bf16[128,3712]{1,0:T(8,128)(2,1)S(1)} %copy-done.1, f32[8,3712]{1,0:T(8,128)S(1)} %pad_convert_fusion.halo_ref, bf16[128,3712]{1,0:T(8,128)(2,1)S(1)} %get-tuple-element.28.mix_ref, ...), custom_call_target="tpu_custom_call" | custom-call | tf_op jit(solution)/shard_map/pallas_call | solution.py:451
  101.5 14.4 %shard_map.131 = (f32[32,8,128]{2,1,0:T(8,128)S(1)}, f32[8,3712]{1,0:T(8,128)S(1)}) custom-call(f32[32,8,128]{2,1,0:T(8,128)S(1)} %get-tuple-element.43.part_ref, f32[8,3712]{1,0:T(8,128)S(1)} %get-tuple-element.44.head_ref), custom_call_target="tpu_custom_call" | custom-call | tf_op jit(solution)/shard_map/pallas_call | solution.py:451
  115.9 0.6 slice_bitcast_fusion
  116.5 0.6 slice_reduce_fusion
  117.2 0.5 slice_bitcast_fusion.1
  117.7 0.7 copy.15
  118.4 0.7 fusion
  (8 shorter events, 0.1 us)
Async XLA Ops:
  1.5 4.6 %collective-permute-start = (bf16[3,3712]{1,0:T(4,128)(2,1)S(1)}, bf16[3,3712]{1,0:T(4,128)(2,1)S(1)}, u32[]{:S(2)}, u32[]{:S(2)}) collective-permute-start(bf16[3,3712]{1,0:T(4,128)(2,1)S(1)} %slice.18), channel_id=1, source_target_pairs={{0,1},{1,2},{2,3},{3,4},{4,5},{5,6},{6,7},{7,8},{8,9},{9,10},{10,1... | collective-permute-start | bytes 66824 | tf_op jit(solution)/shard_map/ppermute | solution.py:495
  6.1 1.2 %copy-start = (bf16[128,3712]{1,0:T(8,128)(2,1)S(1)}, bf16[128,3712]{1,0:T(8,128)(2,1)}, u32[]{:S(2)}) copy-start(bf16[128,3712]{1,0:T(8,128)(2,1)} %x_ref.3) | copy-start | bytes 2850820
  7.3 0.8 copy-start.5
  8.2 32.8 %copy-start.3 = (bf16[128,3584]{1,0:T(8,128)(2,1)S(1)}, bf16[128,3584]{1,0:T(8,128)(2,1)}, u32[]{:S(2)}) copy-start(bf16[128,3584]{1,0:T(8,128)(2,1)} %z_ref.1) | copy-start | bytes 2752516
  40.9 1.2 copy-start.4
  42.1 40.2 %copy-start.1 = (bf16[128,3712]{1,0:T(8,128)(2,1)S(1)}, bf16[128,3712]{1,0:T(8,128)(2,1)}, u32[]{:S(2)}) copy-start(bf16[128,3712]{1,0:T(8,128)(2,1)} %x_ref.3) | copy-start | bytes 2850820
  82.3 1.5 %copy-start.2 = (f32[128,3584]{1,0:T(8,128)S(1)}, f32[128,3584]{1,0:T(8,128)}, u32[]{:S(2)}) copy-start(f32[128,3584]{1,0:T(8,128)} %get-tuple-element.34.gmix_ref) | copy-start | bytes 5505028
where the time goes:
time: 120 us; the launch traced here: 119 us
  Pallas kernels  105 us (88%)
  local copies, waits for them, and re-layouts  10.3 us (9%)
  starting transfers between devices  2.36 us (2%)
    pallas_call x6, Pallas kernels, call(): pl.pallas_call(kernel, out_shape=[jax.ShapeDtypeStruct(shape, dtype) for...  105 us
    unnamed x14, local copies, waits for them, and re-layouts  6.21 us
  transfers between devices with their start and end apart: 1, of which 0 were waited for; matrix products, arithmetic and copies ran while one was open for 2% of the time, Pallas kernels for 0%

commit v1 on v0

--- a/solution.py
+++ b/solution.py
@@ -89,10 +89,8 @@
     return ref[pl.ds(4 * k, 4)].reshape(DSTATE, LANES)
 
 
-def forward_kernel(x_ref, halo_ref, dt_ref, alog_ref, w_ref, mix_ref, end_ref, total_ref, lanes_ref, run_t, step_t):
+def forward_part(x_ref, halo_ref, w_ref, run_t, step_t, mix_ref, end_ref, lanes_ref):
     tiles = x_ref.shape[1] // LANES - 1
-    _, _, running = steps_of(dt_ref, alog_ref, run_t, step_t)
-    total_ref[...] = jnp.broadcast_to(running[-1:], total_ref.shape)
     lanes_ref[...] = jnp.zeros_like(lanes_ref)
 
     def mixin(k):
@@ -113,24 +111,39 @@
         end_ref[pl.ds(4 * k, 4)] = ended[:DSTATE].reshape(4, 16, LANES).astype(BF16)
         return carry
 
-    lax.fori_loop(0, tiles, body, 0)
+    lax.fori_loop(0, tiles, body, 0, unroll=2)
     spare = end_ref.shape[0] - 4 * tiles
     if spare:
         end_ref[4 * tiles :] = jnp.zeros((spare, 16, LANES), BF16)
 
 
-def middle_kernel(
-    mix_ref, z_ref, dt_ref, alog_ref, gain_ref, out_ref, start_ref,
-    normed_ref, gz_ref, gmix_ref, gstart_ref, gain_part_ref, along_ref, gc_ref,
-    run_t, step_t, mixer, sums,
+def scores_of(bc):
+    b_low, c_low, b_high = projections(bc)
+    scores = dot(c_low, b_low, 1, 1)
+    return b_low, c_low, b_high, jnp.concatenate([scores, scores], axis=0)
+
+
+def within_part(begin, end, mix_ref, scores2, run_t, step_t, mixer):
+    lane = iota((LANES, LANES), 1)
+
+    def body(k, carry):
+        at = tile_at(k)
+        scaled, _ = pair_weights(run_t, step_t, k)
+        both = dot((scores2[...] * scaled).astype(BF16), mix_ref[:, at])
+        mixer[:, at] = jnp.where(lane < HEADDIM, both[:LANES], both[LANES:])
+        return carry
+
+    lax.fori_loop(begin, end, body, 0, unroll=2)
+
+
+def middle_part(
+    mix_ref, z_ref, gain_ref, out_ref, start_ref, run_t, mixer,
+    normed_ref, gz_ref, gmix_ref, gstart_ref, gain_part_ref, along_ref, gc_ref, sums,
 ):
     inner = z_ref.shape[1]
     tiles = inner // LANES
-    steps_of(dt_ref, alog_ref, run_t, step_t)
     bc = mix_ref[:, inner : inner + LANES]
-    b_low, c_low, _ = projections(bc)
-    scores = dot(c_low, b_low, 1, 1)
-    scores2 = jnp.concatenate([scores, scores], axis=0)
+    _, c_low, _ = projections(bc)
     lane = iota((LANES, LANES), 1)
     c_both = jnp.where(lane < DSTATE, c_low.astype(F32), bc.astype(F32)).astype(BF16)
 
@@ -143,11 +156,9 @@
 
     def first(k, carry):
         at = tile_at(k)
-        scaled, spread = pair_weights(run_t, step_t, k)
-        both = dot((scores2 * scaled).astype(BF16), mix_ref[:, at])
-        within = jnp.where(lane < HEADDIM, both[:LANES], both[LANES:])
+        spread = columns_of(run_t, k)[-1]
         carried = dot(c_both, parts_of(k))
-        mixed = within + carried * jnp.exp(spread)
+        mixed = mixer[:, at] + carried * jnp.exp(spread)
         mixer[:, at] = mixed
         z = z_ref[:, at].astype(F32)
         gated = mixed * z * sigmoid(z)
@@ -155,7 +166,7 @@
         sums[1] += gated * out_ref[:, at].astype(F32) * gain_ref[0:1, at]
         return carry
 
-    lax.fori_loop(0, tiles, first, 0)
+    lax.fori_loop(0, tiles, first, 0, unroll=2)
     scale = lax.rsqrt(jnp.sum(sums[0], axis=1, keepdims=True) / inner + 1e-05)
     back = scale * scale * scale * (jnp.sum(sums[1], axis=1, keepdims=True) / inner)
     along_ref[...] = jnp.zeros_like(along_ref)
@@ -190,7 +201,7 @@
         gstart_ref[pl.ds(4 * k, 4)] = started[DSTATE:].reshape(4, 16, LANES).astype(BF16)
         return carry
 
-    lax.fori_loop(0, tiles, second, 0)
+    lax.fori_loop(0, tiles, second, 0, unroll=2)
     halves = gc_ref[...]
     gc_ref[...] = jnp.where(lane < DSTATE, 0.0, halves + pltpu.roll(halves, DSTATE, 1))
     spare = gstart_ref.shape[0] - 4 * tiles
@@ -198,23 +209,40 @@
         gstart_ref[4 * tiles :] = jnp.zeros((spare, 16, LANES), BF16)
 
 
-def backward_kernel(
-    x_ref, halo_ref, mix_ref, dt_ref, alog_ref, w_ref, gmix_ref, start_ref, gend_ref, gain_part_ref, along_ref, gc_ref,
+def within_back(begin, end, mix_ref, gmix_ref, scores2, run_t, step_t, gscores, gval, into):
+    lane = iota((LANES, LANES), 1)
+
+    def body(k, carry):
+        at = tile_at(k)
+        values = mix_ref[:, at]
+        gmixer = gmix_ref[:, at]
+        scaled, _ = pair_weights(run_t, step_t, k)
+        weights = (scores2[...] * scaled).astype(BF16)
+        wide = jnp.concatenate([jnp.where(lane < HEADDIM, gmixer, 0.0), jnp.where(lane < HEADDIM, 0.0, gmixer)], axis=0)
+        split = wide.astype(BF16)
+        rest = (wide - split.astype(F32)).astype(BF16)
+        gweights = (dot(split, values, 1, 1) + dot(rest, values, 1, 1)) * scaled
+        gscores[...] += gweights[:LANES] + gweights[LANES:]
+        gvalues = dot(weights, split, 0, 0)
+        into[...] += head_sum(values.astype(F32) * gvalues, k)
+        gval[:, at] = gvalues
+        return carry
+
+    lax.fori_loop(begin, end, body, 0, unroll=2)
+
+
+def backward_part(
+    x_ref, halo_ref, mix_ref, dt_ref, alog_ref, w_ref, start_ref, gend_ref, gain_part_ref, along_ref, gbc,
+    step_ref, decay_ref, run_t, step_t, gscores, gval, into, after, carry_rows,
     gx_ref, head_ref, tail_ref, gdt_ref, part_ref,
-    run_t, step_t, gscores, gbc, into, after, carry_rows,
 ):
-    inner = gmix_ref.shape[1]
+    inner = gval.shape[1]
     tiles = inner // LANES
-    step, log_decay, _ = steps_of(dt_ref, alog_ref, run_t, step_t)
     bc = mix_ref[:, inner : inner + LANES]
-    b_low, c_low, b_high = projections(bc)
-    scores = dot(c_low, b_low, 1, 1)
-    scores2 = jnp.concatenate([scores, scores], axis=0)
-    lane = iota((LANES, LANES), 1)
+    _, c_low, b_high = projections(bc)
     blank = jnp.zeros((DSTATE, LANES), BF16)
-    for ref in (gscores, into, after, carry_rows):
-        ref[...] = jnp.zeros_like(ref)
-    gbc[...] = gc_ref[...]
+    after[...] = jnp.zeros_like(after)
+    carry_rows[...] = jnp.zeros_like(carry_rows)
 
     def conv_back(k, gmixin):
         at = tile_at(k)
@@ -233,36 +261,27 @@
         return [jnp.sum(gpre * ext[5 + o : 5 + o + rows], axis=0, keepdims=True) for o in range(4)]
 
     def body(k, carry):
-        at = tile_at(k)
-        values = mix_ref[:, at]
-        gmixer = gmix_ref[:, at]
-        scaled, spread = pair_weights(run_t, step_t, k)
-        weights = (scores2 * scaled).astype(BF16)
-        wide = jnp.concatenate([jnp.where(lane < HEADDIM, gmixer, 0.0), jnp.where(lane < HEADDIM, 0.0, gmixer)], axis=0)
-        split = wide.astype(BF16)
-        rest = (wide - split.astype(F32)).astype(BF16)
-        gweights = (dot(split, values, 1, 1) + dot(rest, values, 1, 1)) * scaled
-        gscores[...] += gweights[:LANES] + gweights[LANES:]
-        gvalues = dot(weights, split, 0, 0)
+        values = mix_ref[:, tile_at(k)]
+        spread = columns_of(run_t, k)[-1]
         to_end = jnp.exp(spread[-1:] - spread) * columns_of(step_t, k)[-1]
         start, gend = state_tile(start_ref, k), state_tile(gend_ref, k)
         gend_low = jnp.concatenate([gend, blank], axis=0)
         gended = to_end * dot(bc, gend_low)
         values32 = values.astype(F32)
-        into[...] += head_sum(values32 * gvalues, k)
         after[...] += head_sum(values32 * gended, k)
         moved = jnp.sum(start * gend.astype(F32), axis=0, keepdims=True) * jnp.exp(spread[-1:])
         carry_rows[...] += head_sum(jnp.broadcast_to(moved, (16, LANES)), k)
         gbc[...] += dot((values32 * to_end).astype(BF16), gend_low, 1, 1)
-        taps = conv_back(k, gvalues + gended)
+        taps = conv_back(k, gval[:, tile_at(k)] + gended)
         part_ref[k] = jnp.concatenate(taps + [gain_part_ref[k][:1], jnp.zeros((3, LANES), F32)], axis=0)
         return carry
 
-    lax.fori_loop(0, tiles, body, 0)
+    lax.fori_loop(0, tiles, body, 0, unroll=2)
     gscore = gscores[...].astype(BF16)
     rest = (gscores[...] - gscore.astype(F32)).astype(BF16)
     from_scores = dot(gscore, c_low, 0, 0) + dot(gscore, b_high) + dot(rest, c_low, 0, 0) + dot(rest, b_high)
     taps = conv_back(tiles, gbc[...] + from_scores)
+    step, log_decay = step_ref[...], decay_ref[...]
     rows = step.shape[0]
     later = (iota((rows, rows), 0) <= iota((rows, rows), 1)).astype(F32)
     earlier = (iota((rows, rows), 0) > iota((rows, rows), 1)).astype(F32)
@@ -304,9 +323,9 @@
     lax.fori_loop(1, n, one, 0)
 
 
-def exchange_kernel(
+def exchange_part(
     n, axis, reverse, in_ref, lanes_ref, total_ref, out_ref, totals_ref, lanes_near,
-    near, joined, held, decays, back, ret, passed, sems,
+    near, joined, held, decays, back, ret, passed, sems, meanwhile, finish,
 ):
     chips = n // 2
     me = lax.axis_index(axis)
@@ -317,11 +336,6 @@
 
     def peer(d):
         return 2 * lax.rem(chip + d + chips, chips) + core
-
-    barrier = pltpu.get_barrier_semaphore()
-    pl.semaphore_signal(barrier, inc=1, device_id={axis: sibling}, device_id_type=MESH)
-    over_peers(chips, lambda d: pl.semaphore_signal(barrier, inc=1, device_id={axis: peer(d)}, device_id_type=MESH))
-    pl.semaphore_wait(barrier, chips)
 
     def block(j):
         return pl.ds(j * per, per)
@@ -371,6 +385,7 @@
         pair = lax.div(mine + chip * per + i, 4)
         pick = iota((LANES, LANES), 0) == 2 * pair + iota((LANES, LANES), 1) // HEADDIM
         decays[:, i] = jnp.exp(dot_exact(logs, pick.astype(F32))).reshape(chips, 8, LANES)
+    meanwhile()
     over_peers(chips, lambda d: outgoing(d).wait())
 
     def advance(step, state):
@@ -390,6 +405,7 @@
 
     over_peers(chips, lambda d: returning(d).start())
     ret[block(chip)] = back[0]
+    finish()
     over_peers(chips, lambda d: returning(d).wait_send())
     over_peers(chips, lambda d: arriving(d).wait_recv())
 
@@ -411,8 +427,8 @@
     to_peer(passed, out_ref.at[pl.ds((1 - core) * half, half)], sems.at[6, 0], sems.at[7, 0], axis, sibling).wait_recv()
 
 
-def total_kernel(n, axis, part_ref, head_ref, out_ref, rows_ref, held, sems):
-    me = greet_all(axis, n)
+def total_part(n, axis, part_ref, head_ref, out_ref, rows_ref, held, sems):
+    me = lax.axis_index(axis)
     per = part_ref.shape[0] // n
 
     def block(j):
@@ -446,39 +462,66 @@
     rim.wait()
 
 
-def call(kernel, operands, outs, scratch, **params):
-    whole = pl.BlockSpec(memory_space=pltpu.VMEM)
-    return pl.pallas_call(
-        kernel,
-        out_shape=[jax.ShapeDtypeStruct(shape, dtype) for shape, dtype in outs],
-        in_specs=[whole] * len(operands),
-        out_specs=[whole] * len(outs),
-        scratch_shapes=scratch,
-        compiler_params=pltpu.CompilerParams(vmem_limit_bytes=VMEM_LIMIT, **params),
-    )(*operands)
-
-
-def exchange(axis, n, reverse, tiles, lanes, totals, lanes_near=None):
-    chips, half = n // 2, tiles.shape[0] // 2
-    per = half // chips
-    kept = BF16 if reverse else F32
-    near, joined, ret, passed = [pltpu.VMEM((half, 16, LANES), held_as) for held_as in (BF16, BF16, kept, kept)]
-    slots, back = [pltpu.VMEM((chips, per, 16, LANES), held_as) for held_as in (BF16, kept)]
-    scratch = [
-        near, joined, slots, pltpu.VMEM((chips, per, 8, LANES), F32), back, ret, passed,
-        pltpu.SemaphoreType.DMA((8, chips)),
-    ]
-    outs = [(tiles.shape, kept)]
-    operands = [tiles, lanes, totals]
-    if reverse:
-        operands.append(lanes_near)
-
-        def kernel(in_ref, lanes_ref, totals_ref, near_ref, out_ref, *rest):
-            exchange_kernel(n, axis, True, in_ref, lanes_ref, None, out_ref, totals_ref, near_ref, *rest)
-    else:
-        kernel = functools.partial(exchange_kernel, n, axis, False)
-        outs += [((chips + 1, 8, LANES), F32), (lanes.shape, F32)]
-    return call(kernel, operands, outs, scratch, collective_id=1 + reverse, has_side_effects=True)
+def whole_kernel(
+    n, axis,
+    x_ref, z_ref, dt_ref, alog_ref, w_ref, gain_ref, out_ref,
+    normed_ref, gx_ref, gz_ref, gdt_ref, sums_ref,
+    rim, halo, run_t, step_t, step_ref, decay_ref, mix, scores2, mixer, gmix, gval,
+    ended, gstart, start, gend, lanes, lanes_near, total, totals,
+    gain_part, along, gc, norm_sums, gscores, into, after, carry_rows,
+    part, head, tail, back_rows, total_held, rim_sems, total_sems, *states,
+):
+    rows, inner = z_ref.shape
+    tiles = inner // LANES
+    middle = tiles // 4 * 2
+    me = greet_all(axis, n)
+    last = to_peer(x_ref.at[rows - 16 :], rim, rim_sems.at[0], rim_sems.at[1], axis, lax.rem(me + 1, n))
+    last.start()
+    step, log_decay, running = steps_of(dt_ref, alog_ref, run_t, step_t)
+    step_ref[...] = step
+    decay_ref[...] = log_decay
+    total[...] = jnp.broadcast_to(running[-1:], total.shape)
+    last.wait()
+    halo[...] = jnp.where(me > 0, rim[...].astype(F32)[8:], 0.0)
+    forward_part(x_ref, halo, w_ref, run_t, step_t, mix, ended, lanes)
+    scores2[...] = scores_of(mix[:, inner : inner + LANES])[3]
+
+    def within(begin, end):
+        return lambda: within_part(begin, end, mix, scores2, run_t, step_t, mixer)
+
+    exchange_part(
+        n, axis, False, ended, lanes, total, start, totals, lanes_near, *states[:8],
+        within(0, middle), within(middle, tiles),
+    )
+    middle_part(
+        mix, z_ref, gain_ref, out_ref, start, run_t, mixer,
+        normed_ref, gz_ref, gmix, gstart, gain_part, along, gc, norm_sums,
+    )
+    gscores[...] = jnp.zeros_like(gscores)
+    into[...] = jnp.zeros_like(into)
+
+    def back(begin, end):
+        return lambda: within_back(begin, end, mix, gmix, scores2, run_t, step_t, gscores, gval, into)
+
+    exchange_part(
+        n, axis, True, gstart, lanes, None, gend, totals, lanes_near, *states[8:],
+        back(0, middle), back(middle, tiles),
+    )
+    backward_part(
+        x_ref, halo, mix, dt_ref, alog_ref, w_ref, start, gend, gain_part, along, gc,
+        step_ref, decay_ref, run_t, step_t, gscores, gval, into, after, carry_rows,
+        gx_ref, head, tail, gdt_ref, part,
+    )
+    total_part(n, axis, part, head, sums_ref, back_rows, total_held, total_sems)
+
+    def mend(k, carry):
+        at = tile_at(k)
+        borrowed = jnp.where((iota((8, LANES), 0) < 3) & (me < n - 1), back_rows[:, at], 0.0)
+        moved = jnp.concatenate([jnp.zeros((8, LANES), F32), pltpu.roll(borrowed, 5, 0)], axis=0)
+        gx_ref[rows - 16 :, at] = (tail[:, at] + moved).astype(BF16)
+        return carry
+
+    lax.fori_loop(0, tiles + 1, mend, 0)
 
 
 def on_device(xbc_raw, gate_z, dt_raw, a_log, conv_weight, norm_gain, grad_out):
@@ -492,46 +535,48 @@
     state_tiles = -(-4 * tiles // unit) * unit
     lane_rows = -(-state_tiles // 32) * 8
     part_tiles = -(-(tiles + 1) // n) * n
-    rim = lax.ppermute(xbc_raw[rows - 3 :], axis, [(i, i + 1) for i in range(n - 1)])
-    halo = jnp.pad(rim.astype(F32), ((5, 0), (0, 0)))
     dt = jnp.pad(dt_raw, ((0, 0), (0, LANES - heads)))
     alog = jnp.pad(a_log, (0, LANES - heads))[None]
-    per_head = [pltpu.VMEM((LANES, rows), F32)] * 2
-    square = pltpu.VMEM((rows, LANES), F32)
-
-    mixin, ended, total, lanes = call(
-        forward_kernel, (xbc_raw, halo, dt, alog, conv_weight),
-        [((rows, channels), BF16), ((state_tiles, 16, LANES), BF16), ((8, LANES), F32), ((lane_rows, LANES), F32)], per_head,
-    )
-    start, totals, lanes_near = exchange(axis, n, False, ended, lanes, total)
-    normed, grad_z, gmixer, gstart, gain_part, along, gc = call(
-        middle_kernel, (mixin, gate_z, dt, alog, norm_gain[None], grad_out, start),
-        [
-            ((rows, inner), BF16), ((rows, inner), BF16), ((rows, inner), F32),
-            ((state_tiles, 16, LANES), BF16), ((tiles, 8, LANES), F32), ((rows, LANES), F32),
-            ((rows, LANES), F32),
+    chips, half = n // 2, state_tiles // 2
+    per = half // chips
+    vmem = pltpu.VMEM
+    square = vmem((rows, LANES), F32)
+    wide = vmem((rows, inner), F32)
+
+    def states(kept):
+        return [
+            vmem((half, 16, LANES), BF16), vmem((half, 16, LANES), BF16), vmem((chips, per, 16, LANES), BF16),
+            vmem((chips, per, 8, LANES), F32), vmem((chips, per, 16, LANES), kept),
+            vmem((half, 16, LANES), kept), vmem((half, 16, LANES), kept), pltpu.SemaphoreType.DMA((8, chips)),
+        ]
+
+    scratch = [
+        vmem((16, channels), BF16), vmem((8, channels), F32), vmem((LANES, rows), F32), vmem((LANES, rows), F32),
+        square, square, vmem((rows, channels), BF16), vmem((2 * rows, LANES), F32), wide, wide, wide,
+        vmem((state_tiles, 16, LANES), BF16), vmem((state_tiles, 16, LANES), BF16),
+        vmem((state_tiles, 16, LANES), F32), vmem((state_tiles, 16, LANES), BF16),
+        vmem((lane_rows, LANES), F32), vmem((lane_rows, LANES), F32),
+        vmem((8, LANES), F32), vmem((chips + 1, 8, LANES), F32),
+        vmem((tiles, 8, LANES), F32), square, square, vmem((2, rows, LANES), F32),
+        square, square, square, vmem((16, LANES), F32),
+        vmem((part_tiles, 8, LANES), F32), vmem((8, channels), F32), vmem((16, channels), F32),
+        vmem((8, channels), F32), vmem((n, part_tiles // n, 8, LANES), F32),
+        pltpu.SemaphoreType.DMA((2,)), pltpu.SemaphoreType.DMA((4, n)),
+        *states(F32), *states(BF16),
+    ]
+    whole = pl.BlockSpec(memory_space=pltpu.VMEM)
+    normed, grad_xbc, grad_z, gdt, sums = pl.pallas_call(
+        functools.partial(whole_kernel, n, axis),
+        out_shape=[
+            jax.ShapeDtypeStruct((rows, inner), BF16), jax.ShapeDtypeStruct((rows, channels), BF16),
+            jax.ShapeDtypeStruct((rows, inner), BF16), jax.ShapeDtypeStruct((rows, LANES), F32),
+            jax.ShapeDtypeStruct((part_tiles, 8, LANES), F32),
         ],
-        per_head + [pltpu.VMEM((rows, inner), F32), pltpu.VMEM((2, rows, LANES), F32)],
-    )
-    (gend,) = exchange(axis, n, True, gstart, lanes, totals, lanes_near)
-    gx, head, tail, gdt, part = call(
-        backward_kernel,
-        (xbc_raw, halo, mixin, dt, alog, conv_weight, gmixer, start, gend, gain_part, along, gc),
-        [
-            ((rows, channels), BF16), ((8, channels), F32), ((16, channels), F32),
-            ((rows, LANES), F32), ((part_tiles, 8, LANES), F32),
-        ],
-        per_head + [square] * 4 + [pltpu.VMEM((16, LANES), F32)],
-    )
-    sums, back_rows = call(
-        functools.partial(total_kernel, n, axis), (part, head),
-        [((part_tiles, 8, LANES), F32), ((8, channels), F32)],
-        [pltpu.VMEM((n, part_tiles // n, 8, LANES), F32), pltpu.SemaphoreType.DMA((4, n))],
-        collective_id=3, has_side_effects=True,
-    )
-    borrowed = jnp.where(lax.axis_index(axis) < n - 1, back_rows[:3], 0.0)
-    fixed = (tail + jnp.pad(borrowed, ((13, 0), (0, 0)))).astype(BF16)
-    grad_xbc = lax.dynamic_update_slice(gx, fixed, (rows - 16, 0))
+        in_specs=[whole] * 7,
+        out_specs=[whole] * 5,
+        scratch_shapes=scratch,
+        compiler_params=pltpu.CompilerParams(vmem_limit_bytes=VMEM_LIMIT, collective_id=1, has_side_effects=True),
+    )(xbc_raw, gate_z, dt, alog, conv_weight, norm_gain[None], grad_out)
     conv_total = sums[: tiles + 1, :4].transpose(1, 0, 2).reshape(4, channels)
     return (
         normed, grad_xbc, grad_z, gdt[:, :heads], conv_total,

time: 120 us -> 96.5 us (0.80)
  Pallas kernels: 105 us -> 84.5 us
  starting transfers between devices: 2.36 us -> 0 us
    pallas_call x6 -> x1, Pallas kernels: 105 us -> 84.5 us  [on_device(): pl.pallas_call(functools.partial(whole_kernel, n, axis), out_shape=[jax.S...]
    unnamed x14 -> x17, local copies, waits for them, and re-layouts: 6.21 us -> 9.18 us
    ppermute x1 -> x0, starting transfers between devices: 2.36 us -> none  [on_device(): lax.ppermute(xbc_raw[rows - 3:], axis, [(i, i + 1) for i in range(n - 1)])]
  transfers between devices with their start and end apart: 1 -> 0, of which waited for: 0 -> 0; matrix products, arithmetic and copies ran while one was open for 2% -> 0% of each run, Pallas kernels for 0% -> 0%
where the time goes in v1:
time: 96.5 us; the launch traced here: 96.1 us
  Pallas kernels  84.5 us (88%)
  local copies, waits for them, and re-layouts  11 us (11%)
    pallas_call x1, Pallas kernels, on_device(): pl.pallas_call(functools.partial(whole_kernel, n, axis), out_shape=[jax.S...  84.5 us
    unnamed x17, local copies, waits for them, and re-layouts  9.18 us

profile of v1, /device:TPU:0, one launch (start us, length us, event | category | flops | bytes accessed | tf_op | source)
XLA Modules:
  0.0 96.1 jit_solution(4732732634248128792)
XLA Ops:
  0.6 0.8 copy.14
  1.5 0.0 copy-start.4
  1.5 0.0 copy-start.3
  1.5 0.7 copy-done.4
  2.2 0.0 copy-start.5
  2.2 0.6 copy-done.5
  2.9 0.0 copy-done.3
  2.9 0.0 copy-start
  2.9 1.2 %copy-done = bf16[128,3712]{1,0:T(8,128)(2,1)S(1)} copy-done((bf16[128,3712]{1,0:T(8,128)(2,1)S(1)}, bf16[128,3712]{1,0:T(8,128)(2,1)}, u32[]{:S(2)}) %copy-start) | copy-done | bytes 950296
  4.1 0.0 copy-start.1
  4.1 1.2 %copy-done.1 = bf16[128,3584]{1,0:T(8,128)(2,1)S(1)} copy-done((bf16[128,3584]{1,0:T(8,128)(2,1)S(1)}, bf16[128,3584]{1,0:T(8,128)(2,1)}, u32[]{:S(2)}) %copy-start.1) | copy-done | bytes 917528
  5.2 0.0 copy-start.2
  5.2 1.2 %copy-done.2 = bf16[128,3584]{1,0:T(8,128)(2,1)S(1)} copy-done((bf16[128,3584]{1,0:T(8,128)(2,1)S(1)}, bf16[128,3584]{1,0:T(8,128)(2,1)}, u32[]{:S(2)}) %copy-start.2) | copy-done | bytes 917528
  6.4 84.5 %shard_map.126 = (bf16[128,3584]{1,0:T(8,128)(2,1)S(1)}, bf16[128,3712]{1,0:T(8,128)(2,1)S(1)}, bf16[128,3584]{1,0:T(8,128)(2,1)S(1)}, f32[128,128]{1,0:T(8,128)S(1)}, f32[32,8,128]{2,1,0:T(8,128)S(1)}) custom-call(bf16[128,3712]{1,0:T(8,128)(2,1)S(1)} %copy-done, bf16[128,3584]{1,0:T(8,128)(2,1)S(1)} %copy-done.1, f32[128,128]{1,0:T(8,128)S(1)} %pad.8.dt_ref, ...), custom_call_target="tpu_custom_call" | custom-call | tf_op jit(solution)/shard_map/pallas_call | solution.py:568
  90.9 0.6 slice_bitcast_fusion
  91.5 0.6 slice_reduce_fusion
  92.2 0.5 slice_bitcast_fusion.1
  92.7 0.7 copy.15
  93.4 0.9 copy.19
  94.3 0.9 copy.20
  95.2 0.9 copy.21
  (3 shorter events, 0.0 us)
Async XLA Ops:
  1.5 0.7 copy-start.4
  1.5 1.4 %copy-start.3 = (f32[4,3712]{1,0:T(4,128)S(1)}, f32[4,3712]{1,0:T(4,128)}, u32[]{:S(2)}) copy-start(f32[4,3712]{1,0:T(4,128)} %w_ref.1) | copy-start | bytes 178180
  2.2 0.7 copy-start.5
  2.9 1.2 %copy-start = (bf16[128,3712]{1,0:T(8,128)(2,1)S(1)}, bf16[128,3712]{1,0:T(8,128)(2,1)}, u32[]{:S(2)}) copy-start(bf16[128,3712]{1,0:T(8,128)(2,1)} %x_ref.1) | copy-start | bytes 2850820
  4.1 1.2 %copy-start.1 = (bf16[128,3584]{1,0:T(8,128)(2,1)S(1)}, bf16[128,3584]{1,0:T(8,128)(2,1)}, u32[]{:S(2)}) copy-start(bf16[128,3584]{1,0:T(8,128)(2,1)} %z_ref.1) | copy-start | bytes 2752516
  5.2 1.2 %copy-start.2 = (bf16[128,3584]{1,0:T(8,128)(2,1)S(1)}, bf16[128,3584]{1,0:T(8,128)(2,1)}, u32[]{:S(2)}) copy-start(bf16[128,3584]{1,0:T(8,128)(2,1)} %out_ref.1) | copy-start | bytes 2752516

commit v2 on v1

--- a/solution.py
+++ b/solution.py
@@ -63,11 +63,11 @@
 
 
 def pair_weights(run_t, step_t, k):
-    low, high, low_t, high_t, spread = columns_of(run_t, k)
+    low, high, low_t, high_t, _ = columns_of(run_t, k)
     causal = iota((LANES, LANES), 0) >= iota((LANES, LANES), 1)
     gaps = [jnp.where(causal, a - b, -1e30) for a, b in ((low_t, low), (high_t, high))]
     scaled = [jnp.exp(gap) * step_t[pl.ds(2 * k + i, 1), :] for i, gap in enumerate(gaps)]
-    return jnp.concatenate(scaled, axis=0), spread
+    return jnp.concatenate(scaled, axis=0)
 
 
 def projections(bc):
@@ -89,7 +89,7 @@
     return ref[pl.ds(4 * k, 4)].reshape(DSTATE, LANES)
 
 
-def forward_part(x_ref, halo_ref, w_ref, run_t, step_t, mix_ref, end_ref, lanes_ref):
+def forward_part(x_ref, halo_ref, w_ref, run_t, step_t, mix_ref, end_ref, lanes_ref, grown, to_ends):
     tiles = x_ref.shape[1] // LANES - 1
     lanes_ref[...] = jnp.zeros_like(lanes_ref)
 
@@ -106,6 +106,8 @@
         mixed = mixin(k)
         spread = columns_of(run_t, k)[-1]
         to_end = jnp.exp(spread[-1:] - spread) * columns_of(step_t, k)[-1]
+        grown[:, tile_at(k)] = jnp.exp(spread)
+        to_ends[:, tile_at(k)] = to_end
         lanes_ref[pl.ds(k, 1), :] = spread[-1:]
         ended = dot(bc, (mixed.astype(F32) * to_end).astype(BF16), 0, 0)
         end_ref[pl.ds(4 * k, 4)] = ended[:DSTATE].reshape(4, 16, LANES).astype(BF16)
@@ -123,12 +125,13 @@
     return b_low, c_low, b_high, jnp.concatenate([scores, scores], axis=0)
 
 
-def within_part(begin, end, mix_ref, scores2, run_t, step_t, mixer):
+def within_part(begin, end, mix_ref, scores2, run_t, step_t, mixer, scaled_ref):
     lane = iota((LANES, LANES), 1)
 
     def body(k, carry):
         at = tile_at(k)
-        scaled, _ = pair_weights(run_t, step_t, k)
+        scaled = pair_weights(run_t, step_t, k)
+        scaled_ref[k] = scaled
         both = dot((scores2[...] * scaled).astype(BF16), mix_ref[:, at])
         mixer[:, at] = jnp.where(lane < HEADDIM, both[:LANES], both[LANES:])
         return carry
@@ -137,7 +140,7 @@
 
 
 def middle_part(
-    mix_ref, z_ref, gain_ref, out_ref, start_ref, run_t, mixer,
+    mix_ref, z_ref, gain_ref, out_ref, start_ref, grown, mixer,
     normed_ref, gz_ref, gmix_ref, gstart_ref, gain_part_ref, along_ref, gc_ref, sums,
 ):
     inner = z_ref.shape[1]
@@ -156,9 +159,8 @@
 
     def first(k, carry):
         at = tile_at(k)
-        spread = columns_of(run_t, k)[-1]
         carried = dot(c_both, parts_of(k))
-        mixed = mixer[:, at] + carried * jnp.exp(spread)
+        mixed = mixer[:, at] + carried * grown[:, at]
         mixer[:, at] = mixed
         z = z_ref[:, at].astype(F32)
         gated = mixed * z * sigmoid(z)
@@ -174,7 +176,6 @@
 
     def second(k, carry):
         at = tile_at(k)
-        spread = columns_of(run_t, k)[-1]
         mixed = mixer[:, at]
         z = z_ref[:, at].astype(F32)
         gate = sigmoid(z)
@@ -192,7 +193,7 @@
         gmix_ref[:, at] = exact
         wide = gmixer.astype(F32)
         along_ref[...] += head_sum(wide * mixed, k)
-        decayed = exact * jnp.exp(spread)
+        decayed = exact * grown[:, at]
         high = decayed.astype(BF16)
         low = (decayed - high.astype(F32)).astype(BF16)
         placed = parts_of(k)
@@ -209,14 +210,14 @@
         gstart_ref[4 * tiles :] = jnp.zeros((spare, 16, LANES), BF16)
 
 
-def within_back(begin, end, mix_ref, gmix_ref, scores2, run_t, step_t, gscores, gval, into):
+def within_back(begin, end, mix_ref, gmix_ref, scores2, scaled_ref, gscores, gval, into):
     lane = iota((LANES, LANES), 1)
 
     def body(k, carry):
         at = tile_at(k)
         values = mix_ref[:, at]
         gmixer = gmix_ref[:, at]
-        scaled, _ = pair_weights(run_t, step_t, k)
+        scaled = scaled_ref[k]
         weights = (scores2[...] * scaled).astype(BF16)
         wide = jnp.concatenate([jnp.where(lane < HEADDIM, gmixer, 0.0), jnp.where(lane < HEADDIM, 0.0, gmixer)], axis=0)
         split = wide.astype(BF16)
@@ -233,7 +234,7 @@
 
 def backward_part(
     x_ref, halo_ref, mix_ref, dt_ref, alog_ref, w_ref, start_ref, gend_ref, gain_part_ref, along_ref, gbc,
-    step_ref, decay_ref, run_t, step_t, gscores, gval, into, after, carry_rows,
+    step_ref, decay_ref, grown, to_ends, gscores, gval, into, after, carry_rows,
     gx_ref, head_ref, tail_ref, gdt_ref, part_ref,
 ):
     inner = gval.shape[1]
@@ -262,14 +263,13 @@
 
     def body(k, carry):
         values = mix_ref[:, tile_at(k)]
-        spread = columns_of(run_t, k)[-1]
-        to_end = jnp.exp(spread[-1:] - spread) * columns_of(step_t, k)[-1]
+        to_end = to_ends[:, tile_at(k)]
         start, gend = state_tile(start_ref, k), state_tile(gend_ref, k)
         gend_low = jnp.concatenate([gend, blank], axis=0)
         gended = to_end * dot(bc, gend_low)
         values32 = values.astype(F32)
         after[...] += head_sum(values32 * gended, k)
-        moved = jnp.sum(start * gend.astype(F32), axis=0, keepdims=True) * jnp.exp(spread[-1:])
+        moved = jnp.sum(start * gend.astype(F32), axis=0, keepdims=True) * grown[:, tile_at(k)][-1:]
         carry_rows[...] += head_sum(jnp.broadcast_to(moved, (16, LANES)), k)
         gbc[...] += dot((values32 * to_end).astype(BF16), gend_low, 1, 1)
         taps = conv_back(k, gval[:, tile_at(k)] + gended)
@@ -469,11 +469,17 @@
     rim, halo, run_t, step_t, step_ref, decay_ref, mix, scores2, mixer, gmix, gval,
     ended, gstart, start, gend, lanes, lanes_near, total, totals,
     gain_part, along, gc, norm_sums, gscores, into, after, carry_rows,
-    part, head, tail, back_rows, total_held, rim_sems, total_sems, *states,
+    part, head, tail, back_rows, grown, to_ends, scaled, z_held, out_held, fetch_sems, total_held, rim_sems, total_sems, *states,
 ):
     rows, inner = z_ref.shape
     tiles = inner // LANES
     middle = tiles // 4 * 2
+    fetches = [
+        pltpu.make_async_copy(z_ref, z_held, fetch_sems.at[0]),
+        pltpu.make_async_copy(out_ref, out_held, fetch_sems.at[1]),
+    ]
+    for fetch in fetches:
+        fetch.start()
     me = greet_all(axis, n)
     last = to_peer(x_ref.at[rows - 16 :], rim, rim_sems.at[0], rim_sems.at[1], axis, lax.rem(me + 1, n))
     last.start()
@@ -483,25 +489,27 @@
     total[...] = jnp.broadcast_to(running[-1:], total.shape)
     last.wait()
     halo[...] = jnp.where(me > 0, rim[...].astype(F32)[8:], 0.0)
-    forward_part(x_ref, halo, w_ref, run_t, step_t, mix, ended, lanes)
+    forward_part(x_ref, halo, w_ref, run_t, step_t, mix, ended, lanes, grown, to_ends)
     scores2[...] = scores_of(mix[:, inner : inner + LANES])[3]
 
     def within(begin, end):
-        return lambda: within_part(begin, end, mix, scores2, run_t, step_t, mixer)
+        return lambda: within_part(begin, end, mix, scores2, run_t, step_t, mixer, scaled)
 
     exchange_part(
         n, axis, False, ended, lanes, total, start, totals, lanes_near, *states[:8],
         within(0, middle), within(middle, tiles),
     )
+    for fetch in fetches:
+        fetch.wait()
     middle_part(
-        mix, z_ref, gain_ref, out_ref, start, run_t, mixer,
+        mix, z_held, gain_ref, out_held, start, grown, mixer,
         normed_ref, gz_ref, gmix, gstart, gain_part, along, gc, norm_sums,
     )
     gscores[...] = jnp.zeros_like(gscores)
     into[...] = jnp.zeros_like(into)
 
     def back(begin, end):
-        return lambda: within_back(begin, end, mix, gmix, scores2, run_t, step_t, gscores, gval, into)
+        return lambda: within_back(begin, end, mix, gmix, scores2, scaled, gscores, gval, into)
 
     exchange_part(
         n, axis, True, gstart, lanes, None, gend, totals, lanes_near, *states[8:],
@@ -509,7 +517,7 @@
     )
     backward_part(
         x_ref, halo, mix, dt_ref, alog_ref, w_ref, start, gend, gain_part, along, gc,
-        step_ref, decay_ref, run_t, step_t, gscores, gval, into, after, carry_rows,
+        step_ref, decay_ref, grown, to_ends, gscores, gval, into, after, carry_rows,
         gx_ref, head, tail, gdt_ref, part,
     )
     total_part(n, axis, part, head, sums_ref, back_rows, total_held, total_sems)
@@ -560,11 +568,14 @@
         vmem((tiles, 8, LANES), F32), square, square, vmem((2, rows, LANES), F32),
         square, square, square, vmem((16, LANES), F32),
         vmem((part_tiles, 8, LANES), F32), vmem((8, channels), F32), vmem((16, channels), F32),
-        vmem((8, channels), F32), vmem((n, part_tiles // n, 8, LANES), F32),
+        vmem((8, channels), F32), wide, wide, vmem((tiles, 2 * rows, LANES), F32),
+        vmem((rows, inner), BF16), vmem((rows, inner), BF16), pltpu.SemaphoreType.DMA((2,)),
+        vmem((n, part_tiles // n, 8, LANES), F32),
         pltpu.SemaphoreType.DMA((2,)), pltpu.SemaphoreType.DMA((4, n)),
         *states(F32), *states(BF16),
     ]
     whole = pl.BlockSpec(memory_space=pltpu.VMEM)
+    away = pl.BlockSpec(memory_space=pl.ANY)
     normed, grad_xbc, grad_z, gdt, sums = pl.pallas_call(
         functools.partial(whole_kernel, n, axis),
         out_shape=[
@@ -572,7 +583,7 @@
             jax.ShapeDtypeStruct((rows, inner), BF16), jax.ShapeDtypeStruct((rows, LANES), F32),
             jax.ShapeDtypeStruct((part_tiles, 8, LANES), F32),
         ],
-        in_specs=[whole] * 7,
+        in_specs=[whole, away, whole, whole, whole, whole, away],
         out_specs=[whole] * 5,
         scratch_shapes=scratch,
         compiler_params=pltpu.CompilerParams(vmem_limit_bytes=VMEM_LIMIT, collective_id=1, has_side_effects=True),

time: 96.5 us -> 97.6 us (1.011)
  Pallas kernels: 84.5 us -> 85.6 us
    pallas_call x1, Pallas kernels: 84.5 us -> 85.6 us  [on_device(): pl.pallas_call(functools.partial(whole_kernel, n, axis), out_shape=[jax.S...]
where the time goes in v2:
time: 97.6 us; the launch traced here: 97.3 us
  Pallas kernels  85.6 us (88%)
  local copies, waits for them, and re-layouts  11 us (11%)
    pallas_call x1, Pallas kernels, on_device(): pl.pallas_call(functools.partial(whole_kernel, n, axis), out_shape=[jax.S...  85.6 us
    unnamed x17, local copies, waits for them, and re-layouts  9.18 us

profile of v2, /device:TPU:0, one launch (start us, length us, event | category | flops | bytes accessed | tf_op | source)
XLA Modules:
  0.0 97.3 jit_solution(6191160899756814911)
XLA Ops:
  0.6 0.8 copy.14
  1.5 0.0 copy-start.4
  1.5 0.0 copy-start.3
  1.5 0.7 copy-done.4
  2.2 0.0 copy-start.5
  2.2 0.6 copy-done.5
  2.9 0.0 copy-done.3
  2.9 0.0 copy-start
  2.9 1.2 %copy-done = bf16[128,3712]{1,0:T(8,128)(2,1)S(1)} copy-done((bf16[128,3712]{1,0:T(8,128)(2,1)S(1)}, bf16[128,3712]{1,0:T(8,128)(2,1)}, u32[]{:S(2)}) %copy-start) | copy-done | bytes 950296
  4.1 0.0 copy-start.1
  4.1 1.2 %copy-done.1 = bf16[128,3584]{1,0:T(8,128)(2,1)S(1)} copy-done((bf16[128,3584]{1,0:T(8,128)(2,1)S(1)}, bf16[128,3584]{1,0:T(8,128)(2,1)}, u32[]{:S(2)}) %copy-start.1) | copy-done | bytes 917528
  5.2 0.0 copy-start.2
  5.2 1.2 %copy-done.2 = bf16[128,3584]{1,0:T(8,128)(2,1)S(1)} copy-done((bf16[128,3584]{1,0:T(8,128)(2,1)S(1)}, bf16[128,3584]{1,0:T(8,128)(2,1)}, u32[]{:S(2)}) %copy-start.2) | copy-done | bytes 917528
  6.4 85.6 %shard_map.126 = (bf16[128,3584]{1,0:T(8,128)(2,1)S(1)}, bf16[128,3712]{1,0:T(8,128)(2,1)S(1)}, bf16[128,3584]{1,0:T(8,128)(2,1)S(1)}, f32[128,128]{1,0:T(8,128)S(1)}, f32[32,8,128]{2,1,0:T(8,128)S(1)}) custom-call(bf16[128,3712]{1,0:T(8,128)(2,1)S(1)} %copy-done, bf16[128,3584]{1,0:T(8,128)(2,1)S(1)} %copy-done.1, f32[128,128]{1,0:T(8,128)S(1)} %pad.8.dt_ref, ...), custom_call_target="tpu_custom_call" | custom-call | tf_op jit(solution)/shard_map/pallas_call | solution.py:579
  92.0 0.6 slice_bitcast_fusion
  92.6 0.6 slice_reduce_fusion
  93.3 0.5 slice_bitcast_fusion.1
  93.8 0.7 copy.15
  94.5 0.9 copy.19
  95.4 0.9 copy.20
  96.3 0.9 copy.21
  (3 shorter events, 0.0 us)
Async XLA Ops:
  1.5 0.7 copy-start.4
  1.5 1.4 %copy-start.3 = (f32[4,3712]{1,0:T(4,128)S(1)}, f32[4,3712]{1,0:T(4,128)}, u32[]{:S(2)}) copy-start(f32[4,3712]{1,0:T(4,128)} %w_ref.1) | copy-start | bytes 178180
  2.2 0.7 copy-start.5
  2.9 1.2 %copy-start = (bf16[128,3712]{1,0:T(8,128)(2,1)S(1)}, bf16[128,3712]{1,0:T(8,128)(2,1)}, u32[]{:S(2)}) copy-start(bf16[128,3712]{1,0:T(8,128)(2,1)} %x_ref.1) | copy-start | bytes 2850820
  4.1 1.2 %copy-start.1 = (bf16[128,3584]{1,0:T(8,128)(2,1)S(1)}, bf16[128,3584]{1,0:T(8,128)(2,1)}, u32[]{:S(2)}) copy-start(bf16[128,3584]{1,0:T(8,128)(2,1)} %z_ref.1) | copy-start | bytes 2752516
  5.2 1.2 %copy-start.2 = (bf16[128,3584]{1,0:T(8,128)(2,1)S(1)}, bf16[128,3584]{1,0:T(8,128)(2,1)}, u32[]{:S(2)}) copy-start(bf16[128,3584]{1,0:T(8,128)(2,1)} %out_ref.1) | copy-start | bytes 2752516

commit v3 on v2

--- a/solution.py
+++ b/solution.py
@@ -14,7 +14,7 @@
 MESH = pl.DeviceIdType.MESH
 F32 = jnp.float32
 BF16 = jnp.bfloat16
-VMEM_LIMIT = 48 * 1024 * 1024
+VMEM_LIMIT = 60 * 1024 * 1024
 
 
 def dot(a, b, ca=1, cb=0):

time: 97.6 us -> 101 us (1.035)
  Pallas kernels: 85.6 us -> 87.6 us
  local copies, waits for them, and re-layouts: 11 us -> 12.3 us
    unnamed x17 -> x15, local copies, waits for them, and re-layouts: 9.18 us -> 6.26 us
    pallas_call x1, Pallas kernels: 85.6 us -> 87.6 us  [on_device(): pl.pallas_call(functools.partial(whole_kernel, n, axis), out_shape=[jax.S...]
where the time goes in v3:
time: 101 us
  Pallas kernels  87.6 us (87%)
  local copies, waits for them, and re-layouts  12.3 us (12%)
    pallas_call x1, Pallas kernels, on_device(): pl.pallas_call(functools.partial(whole_kernel, n, axis), out_shape=[jax.S...  87.6 us
    unnamed x15, local copies, waits for them, and re-layouts  6.26 us

profile of v3, /device:TPU:0, one launch (start us, length us, event | category | flops | bytes accessed | tf_op | source)
XLA Modules:
  0.0 100.5 jit_solution(3224472519989186608)
XLA Ops:
  0.6 0.8 copy.14
  1.5 0.0 copy-start.3
  1.5 0.6 pad.8.dt_ref
  2.1 0.1 copy-done.3
  2.2 0.0 copy-start.4
  2.2 0.6 broadcast_in_dim.7.gain_ref
  2.8 0.0 copy-done.4
  2.9 0.5 pad_bitcast_fusion.alog_ref
  3.4 87.6 %shard_map.126 = (bf16[128,3584]{1,0:T(8,128)(2,1)}, bf16[128,3712]{1,0:T(8,128)(2,1)}, bf16[128,3584]{1,0:T(8,128)(2,1)}, f32[128,128]{1,0:T(8,128)}, f32[32,8,128]{2,1,0:T(8,128)}) custom-call(bf16[128,3712]{1,0:T(8,128)(2,1)} %x_ref.1, bf16[128,3584]{1,0:T(8,128)(2,1)} %z_ref.1, f32[128,128]{1,0:T(8,128)} %pad.8.dt_ref, ...), custom_call_target="tpu_custom_call" | custom-call | tf_op jit(solution)/shard_map/pallas_call | solution.py:579
  90.9 0.0 copy-start.2
  91.0 1.6 %slice_bitcast_fusion = f32[4,3712]{1,0:T(4,128)} fusion(f32[32,8,128]{2,1,0:T(8,128)} %get-tuple-element.16), kind=kLoop, calls=%fused_computation | loop fusion | bytes 118784 | tf_op jit(solution)/shard_map/reshape | solution.py:591
  92.5 1.5 %slice_reduce_fusion = f32[28,128]{1,0:T(8,128)} fusion(f32[32,8,128]{2,1,0:T(8,128)} %get-tuple-element.16), kind=kLoop, calls=%fused_computation.1 | loop fusion | bytes 28672 | tf_op jit(solution)/shard_map/slice | solution.py:594
  94.1 1.2 %slice_bitcast_fusion.1 = f32[56]{0:T(128)} fusion(f32[32,8,128]{2,1,0:T(8,128)} %get-tuple-element.16), kind=kLoop, calls=%fused_computation.2 | loop fusion | bytes 448 | tf_op jit(solution)/shard_map/squeeze | solution.py:594
  95.2 0.0 copy-done.2
  95.2 0.0 copy-start
  95.2 0.7 copy.15
  95.9 2.2 %copy.19 = bf16[128,3584]{1,0:T(8,128)(2,1)} copy(bf16[128,3584]{1,0:T(8,128)(2,1)} %get-tuple-element.31) | data formatting | bytes 1835008
  98.1 0.0 copy-done
  98.1 0.0 copy-start.1
  98.1 0.9 copy.20
  99.0 0.6 copy-done.1
  99.6 0.9 copy.21
Async XLA Ops:
  1.5 0.7 copy-start.3
  2.2 0.7 copy-start.4
  90.9 4.3 %copy-start.2 = (f32[128,128]{1,0:T(8,128)S(1)}, f32[128,128]{1,0:T(8,128)}, u32[]{:S(2)}) copy-start(f32[128,128]{1,0:T(8,128)} %get-tuple-element.15) | copy-start | bytes 196612
  95.2 2.9 %copy-start = (bf16[128,3712]{1,0:T(8,128)(2,1)S(1)}, bf16[128,3712]{1,0:T(8,128)(2,1)}, u32[]{:S(2)}) copy-start(bf16[128,3712]{1,0:T(8,128)(2,1)} %get-tuple-element.32) | copy-start | bytes 2850820
  98.1 1.5 %copy-start.1 = (bf16[128,3584]{1,0:T(8,128)(2,1)S(1)}, bf16[128,3584]{1,0:T(8,128)(2,1)}, u32[]{:S(2)}) copy-start(bf16[128,3584]{1,0:T(8,128)(2,1)} %get-tuple-element.33) | copy-start | bytes 2752516
